TPU v7x, 32 devices: a whole 2x2x4 slice. The times are simulated.
32 devices in a mesh: gx: 4 (over x, core), gy: 8 (over z, y).
Axes of the slice: x: 2, y: 2, z: 4, core: 2. Of those that a mesh axis runs over, the one named last changes fastest.
Arguments:
- coefficients: float32 [3, 16, 128, 128], P(None, 'gx', 'gy'), may hold values from -3 to 3
- fractions: float32 [3, 65536], P(None, ('gx', 'gy')), may hold values from 0 to 1
- targets: float32 [3, 65536], P(None, ('gx', 'gy')), may hold values from -6 to 6
- block_cell: int32 [512], P(('gx', 'gy')), may hold values from 0 to 8191
- block_fill: int32 [512], P(('gx', 'gy')), may hold values from 0 to 128, as said below
Outputs:
- fitted: float32 [3, 16, 128, 128], P(None, 'gx', 'gy')
- losses: float32 [4], replicated
Inputs may be any that keep to these rules, and one draw needn't show every extreme that they name: `block_fill`: in each brick's 16 slots the live blocks come first and the empty ones (fill 0) last; every brick's first block holds 128 samples, and the brick with the most live blocks has all slots live.
All inputs are finite; a program needn't handle non-finite values.
Results may differ from a plain program's by a relative error of at most 0.0001.
Values sent between devices are 32-bit elements; how exact they have to be, the bound alone decides.
A program may use at most 64 MiB of HBM per device.

v0:
```python
import math

import jax
import jax.numpy as jnp
from jax import lax
from jax.sharding import PartitionSpec as P

ITERS = 4


penalty_weight = 0.5
learn_rate = 0.05
beta_one = 0.9
beta_two = 0.999
adam_eps = 0.1


def with_halo(block, sides, width):
    for axis, dim in sides:
        count = lax.axis_size(axis)
        forward = [(i, i + 1) for i in range(count - 1)]
        backward = [(target, source) for source, target in forward]
        low = lax.ppermute(
            lax.slice_in_dim(block, block.shape[dim] - width, None, axis=dim), axis, forward
        )
        high = lax.ppermute(lax.slice_in_dim(block, 0, width, axis=dim), axis, backward)
        block = jnp.concatenate([low, block, high], axis=dim)
    return block


def shifted(value, axis, by):
    length = lax.axis_size(axis)
    pairs = [(i, i + by) for i in range(length) if 0 <= i + by < length]
    return lax.ppermute(value, axis, pairs)


def spline_weights(u):
    one_minus = 1.0 - u
    return jnp.stack(
        [
            one_minus**3 / 6.0,
            (3.0 * u**3 - 6.0 * u**2 + 4.0) / 6.0,
            (-3.0 * u**3 + 3.0 * u**2 + 3.0 * u + 1.0) / 6.0,
            u**3 / 6.0,
        ]
    )


def tensor_basis(fraction):
    full = jnp.einsum(
        "ags,bgs,cgs->gsabc",
        spline_weights(fraction[0]),
        spline_weights(fraction[1]),
        spline_weights(fraction[2]),
        precision=lax.Precision.HIGHEST,
    )
    return full.reshape(full.shape[0], full.shape[1], 64)


def ghosts(coef):
    return with_halo(coef, (("gx", 1), ("gy", 2)), 2)


def fold_x(grad_ext):
    length = grad_ext.shape[1] - 4
    from_below = shifted(grad_ext[:, length + 2 : length + 4], "gx", 1)
    from_above = shifted(grad_ext[:, 0:2], "gx", -1)
    inner = grad_ext[:, 2 : length + 2]
    inner = inner.at[:, 0:2].add(from_below)
    return inner.at[:, length - 2 : length].add(from_above)


def fold_y(grad_ext):
    length = grad_ext.shape[2] - 4
    from_below = shifted(grad_ext[:, :, length + 2 : length + 4], "gy", 1)
    from_above = shifted(grad_ext[:, :, 0:2], "gy", -1)
    inner = grad_ext[:, :, 2 : length + 2]
    inner = inner.at[:, :, 0:2].add(from_below)
    return inner.at[:, :, length - 2 : length].add(from_above)


def shards(coefficients, fractions, targets, block_cell, block_fill):
    cells_x = coefficients.shape[1]
    cells_y = coefficients.shape[2]
    depth = coefficients.shape[3]
    blocks = block_cell.shape[0]
    samples = fractions.shape[1] // blocks
    bricks_x = lax.axis_size("gx")
    bricks_y = lax.axis_size("gy")
    column = lax.axis_index("gx")
    row_no = lax.axis_index("gy")
    grand_total = lax.psum(jnp.sum(block_fill).astype(jnp.float32), ("gx", "gy"))
    ncells = cells_x * bricks_x * cells_y * bricks_y * depth
    data_scale = ncells / grand_total
    group = math.gcd(blocks, 64)
    rounds = blocks // group
    local_x = block_cell // (cells_y * depth)
    local_y = block_cell // depth % cells_y
    local_z = block_cell % depth
    alive = (jnp.arange(samples, dtype=jnp.int32)[None, :] < block_fill[:, None]).astype(
        jnp.float32
    )
    nodes = jnp.arange(64, dtype=jnp.int32)
    off_x, off_y, off_z = (nodes // 16, nodes // 4 % 4, nodes % 4)
    pos_x = column * cells_x + jnp.arange(cells_x + 2, dtype=jnp.int32) - 1
    pos_y = row_no * cells_y + jnp.arange(cells_y + 2, dtype=jnp.int32) - 1
    pos_z = jnp.arange(depth + 2, dtype=jnp.int32) - 1
    inside = (
        ((pos_x >= 0) & (pos_x < cells_x * bricks_x))[:, None, None]
        & ((pos_y >= 0) & (pos_y < cells_y * bricks_y))[None, :, None]
        & ((pos_z >= 0) & (pos_z < depth))[None, None, :]
    ).astype(jnp.float32)
    current = coefficients
    moment = jnp.zeros_like(coefficients)
    second = jnp.zeros_like(coefficients)
    history = []
    for iteration in range(ITERS):
        haloed = ghosts(current)
        extended = jnp.pad(haloed, ((0, 0), (0, 0), (0, 0), (2, 2)))

        def take_patch(a_pos, b_pos, c_pos):
            return lax.dynamic_slice(
                extended, (jnp.int32(0), a_pos + 1, b_pos + 1, c_pos + 1), (3, 4, 4, 4)
            )

        def one_round(turn, carry):
            grad_ext, data_sq = carry
            frac = fractions.reshape(3, group, samples)
            wanted = targets.reshape(3, group, samples)
            patches = jax.vmap(take_patch)(local_x, local_y, local_z).reshape(group, 3, 64)
            basis_mat = tensor_basis(frac)
            predicted = jnp.einsum(
                "gsn,gcn->cgs", basis_mat, patches, precision=lax.Precision.HIGHEST
            )
            misfit = (predicted - wanted) * alive[None]
            data_sq = data_sq + jnp.sum(misfit * misfit)
            term = 2.0 * jnp.einsum(
                "gsn,cgs->cgn", basis_mat, misfit, precision=lax.Precision.HIGHEST
            )
            grad_ext = grad_ext.at[
                :,
                local_x[:, None] + 1 + off_x,
                local_y[:, None] + 1 + off_y,
                local_z[:, None] + 1 + off_z,
            ].add(term)
            return (grad_ext, data_sq)

        start_carry = (jnp.zeros(extended.shape, jnp.float32), jnp.float32(0.0))
        grad_ext, data_sq = lax.fori_loop(0, rounds, one_round, start_carry)
        grad_ext = grad_ext[:, :, :, 2 : depth + 2]
        grad_data = fold_y(fold_x(grad_ext))
        divergence = (
            extended[0, 2 : cells_x + 4, 1 : cells_y + 3, 1 : depth + 3]
            - extended[0, 0 : cells_x + 2, 1 : cells_y + 3, 1 : depth + 3]
            + extended[1, 1 : cells_x + 3, 2 : cells_y + 4, 1 : depth + 3]
            - extended[1, 1 : cells_x + 3, 0 : cells_y + 2, 1 : depth + 3]
            + extended[2, 1 : cells_x + 3, 1 : cells_y + 3, 2 : depth + 4]
            - extended[2, 1 : cells_x + 3, 1 : cells_y + 3, 0 : depth + 2]
        ) / 2.0
        divergence = divergence * inside
        own_div = divergence[1 : cells_x + 1, 1 : cells_y + 1, 1 : depth + 1]
        spread = jnp.sum(own_div * own_div)
        grad_div = jnp.stack(
            [
                penalty_weight
                * (
                    divergence[0:cells_x, 1 : cells_y + 1, 1 : depth + 1]
                    - divergence[2 : cells_x + 2, 1 : cells_y + 1, 1 : depth + 1]
                ),
                penalty_weight
                * (
                    divergence[1 : cells_x + 1, 0:cells_y, 1 : depth + 1]
                    - divergence[1 : cells_x + 1, 2 : cells_y + 2, 1 : depth + 1]
                ),
                penalty_weight
                * (
                    divergence[1 : cells_x + 1, 1 : cells_y + 1, 0:depth]
                    - divergence[1 : cells_x + 1, 1 : cells_y + 1, 2 : depth + 2]
                ),
            ]
        )
        gradient = data_scale * grad_data + grad_div
        summed = lax.psum((data_sq, spread), ("gx", "gy"))
        history.append(summed[0] / grand_total + penalty_weight * summed[1] / ncells)
        moment = beta_one * moment + (1.0 - beta_one) * gradient
        second = beta_two * second + (1.0 - beta_two) * gradient * gradient
        corr_one = 1.0 - beta_one ** (iteration + 1)
        corr_two = 1.0 - beta_two ** (iteration + 1)
        current = current - learn_rate * (moment / corr_one) / (
            jnp.sqrt(second / corr_two) + adam_eps
        )
    losses = jnp.stack(history)
    return (current, losses)


def solution(mesh):
    placed = (
        P(None, "gx", "gy", None),
        P(None, ("gx", "gy")),
        P(None, ("gx", "gy")),
        P(("gx", "gy")),
        P(("gx", "gy")),
    )
    return jax.shard_map(
        shards,
        mesh=mesh,
        in_specs=placed,
        out_specs=(P(None, "gx", "gy", None), P()),
        check_vma=False,
    )
```

profile of v0, /device:TPU:0, one launch (start us, length us, event | category | flops | bytes accessed | tf_op | source)
XLA Modules:
  0.0 497.1 jit_solution(3218400092885038476)
XLA Ops:
  2.9 3.0 collective-permute-start
  13.8 5.5 %collective-permute-start.2 = (f32[3,8,2,128]{3,1,2,0:T(8,128)S(1)}, f32[3,8,2,128]{3,1,2,0:T(8,128)S(1)}, u32[]{:S(2)}, u32[]{:S(2)}) collective-permute-start(f32[3,8,2,128]{3,1,2,0:T(8,128)S(1)} %get-tuple-element.493), channel_id=1, source_target_pairs={{0,1},{1,2},{2,3},{3,4},{4,5},{5,6},{6,7},{8,9},{9,10},{10,11},{11... | collective-permute-start | bytes 73736 | tf_op jit(solution)/shard_map/ppermute | solution.py:23
  19.3 42.0 %psum.63 = f32[]{:T(128)} all-reduce(f32[]{:T(128)S(6)} %convert_element_type.16), channel_id=1, replica_groups=mesh['gx'=4,'gy'=8] {'gx','gy'}, use_global_device_ids=true, to_apply=%region_1.0 | all-reduce | flops 1 | bytes 8 | tf_op jit(solution)/shard_map/psum | solution.py:92
  62.5 43.7 %while.40 = (s32[]{:T(128)}, f32[3,8,20,132]{3,1,2,0:T(8,128)S(1)}, s32[16,4]{0,1:T(4,128)S(1)}, f32[16,3,4,4,4]{4,3,2,1,0:T(4,128)S(1)}, s32[]{:T(128)}) while((s32[]{:T(128)}, f32[3,8,20,132]{3,1,2,0:T(8,128)S(1)}, s32[16,4]{0,1:T(4,128)S(1)}, f32[16,3,4,4,4]{4,3,2,1,0:T(4,128)S(1)}, s32[]{:T(128)}) %tuple.205), condition=%wide.while_cond.16, body=%wide.while_body.16.sunk | while | flops 2 | bytes 50833 | solution.py:122
  63.2 2.0 constant_dynamic-slice_fusion.17
  68.7 2.0 constant_dynamic-slice_fusion.17
  71.4 2.0 constant_dynamic-slice_fusion.17
  74.1 2.0 constant_dynamic-slice_fusion.17
  76.9 2.0 constant_dynamic-slice_fusion.17
  79.6 2.0 constant_dynamic-slice_fusion.17
  82.3 2.0 constant_dynamic-slice_fusion.17
  87.8 2.0 constant_dynamic-slice_fusion.17
  90.5 2.0 constant_dynamic-slice_fusion.17
  96.0 2.0 constant_dynamic-slice_fusion.17
  98.7 2.0 constant_dynamic-slice_fusion.17
  104.2 2.0 constant_dynamic-slice_fusion.17
  109.9 10.8 %scatter_custom_fusion = f32[3,21120]{0,1:T(8,128)} fusion(s32[1024]{0:T(1024)S(1)} %reshape.1316, f32[1024,3]{1,0:T(8,128)S(1)} %bitcast.209, f32[]{:T(128)} %constant.637.clone.1), kind=kCustom, calls=%fused_computation.26 | custom fusion | flops 3072 | bytes 253444
  120.6 6.4 %copy.57 = f32[3,21120]{1,0:T(4,128)S(1)} copy(f32[3,21120]{0,1:T(8,128)} %scatter_custom_fusion) | data formatting | bytes 506880
  131.1 3.8 collective-permute-done.5
  134.9 2.6 collective-permute-start.6
  139.5 4.3 collective-permute-done.7
  145.3 4.0 collective-permute-start.8
  151.5 4.7 collective-permute-start.10
  158.0 43.7 %while.41 = (s32[]{:T(128)}, f32[3,8,20,132]{3,1,2,0:T(8,128)S(1)}, s32[16,4]{0,1:T(4,128)S(1)}, f32[16,3,4,4,4]{4,3,2,1,0:T(4,128)S(1)}, s32[]{:T(128)}) while((s32[]{:T(128)}, f32[3,8,20,132]{3,1,2,0:T(8,128)S(1)}, s32[16,4]{0,1:T(4,128)S(1)}, f32[16,3,4,4,4]{4,3,2,1,0:T(4,128)S(1)}, s32[]{:T(128)}) %tuple.217), condition=%wide.while_cond.17, body=%wide.while_body.17.sunk | while | flops 2 | bytes 50833 | solution.py:122
  204.5 10.8 %scatter_custom_fusion.1 = f32[3,21120]{0,1:T(8,128)} fusion(s32[1024]{0:T(1024)S(1)} %reshape.1316, f32[1024,3]{1,0:T(8,128)S(1)} %bitcast.210, f32[]{:T(128)} %constant.637.clone.1), kind=kCustom, calls=%fused_computation.24 | custom fusion | flops 3072 | bytes 253444
  215.3 6.4 %copy.64 = f32[3,21120]{1,0:T(4,128)S(1)} copy(f32[3,21120]{0,1:T(8,128)} %scatter_custom_fusion.1) | data formatting | bytes 506880
  222.6 2.9 collective-permute-start.12
  227.4 4.5 collective-permute-done.13
  232.0 4.7 collective-permute-start.14
  238.8 5.5 %collective-permute-done.15 = f32[3,4,2,128]{3,1,2,0:T(4,128)S(1)} collective-permute-done((f32[3,4,2,128]{3,1,2,0:T(4,128)S(1)}, f32[3,4,2,128]{3,1,2,0:T(4,128)S(1)}, u32[]{:S(2)}, u32[]{:S(2)}) %collective-permute-start.15) | collective-permute-done | bytes 12320 | tf_op jit(solution)/shard_map/ppermute | solution.py:34
  245.8 4.3 collective-permute-start.16
  252.2 5.4 %collective-permute-start.18 = (f32[3,8,2,128]{3,1,2,0:T(8,128)S(1)}, f32[3,8,2,128]{3,1,2,0:T(8,128)S(1)}, u32[]{:S(2)}, u32[]{:S(2)}) collective-permute-start(f32[3,8,2,128]{3,1,2,0:T(8,128)S(1)} %get-tuple-element.489), channel_id=1, source_target_pairs={{0,1},{1,2},{2,3},{3,4},{4,5},{5,6},{6,7},{8,9},{9,10},{10,11},{11... | collective-permute-start | bytes 73736 | tf_op jit(solution)/shard_map/ppermute | solution.py:23
  259.4 43.7 %while.42 = (s32[]{:T(128)}, f32[3,8,20,132]{3,1,2,0:T(8,128)S(1)}, s32[16,4]{0,1:T(4,128)S(1)}, f32[16,3,4,4,4]{4,3,2,1,0:T(4,128)S(1)}, s32[]{:T(128)}) while((s32[]{:T(128)}, f32[3,8,20,132]{3,1,2,0:T(8,128)S(1)}, s32[16,4]{0,1:T(4,128)S(1)}, f32[16,3,4,4,4]{4,3,2,1,0:T(4,128)S(1)}, s32[]{:T(128)}) %tuple.218), condition=%wide.while_cond.18, body=%wide.while_body.18.sunk | while | flops 2 | bytes 50833 | solution.py:122
  305.9 10.8 %scatter_custom_fusion.2 = f32[3,21120]{0,1:T(8,128)} fusion(s32[1024]{0:T(1024)S(1)} %reshape.1316, f32[1024,3]{1,0:T(8,128)S(1)} %bitcast.211, f32[]{:T(128)} %constant.637.clone.1), kind=kCustom, calls=%fused_computation.22 | custom fusion | flops 3072 | bytes 253444
  316.7 6.4 %copy.70 = f32[3,21120]{1,0:T(4,128)S(1)} copy(f32[3,21120]{0,1:T(8,128)} %scatter_custom_fusion.2) | data formatting | bytes 506880
  323.9 3.1 collective-permute-start.20
  328.9 4.4 collective-permute-done.21
  333.4 4.8 collective-permute-start.22
  340.2 5.5 %collective-permute-done.23 = f32[3,4,2,128]{3,1,2,0:T(4,128)S(1)} collective-permute-done((f32[3,4,2,128]{3,1,2,0:T(4,128)S(1)}, f32[3,4,2,128]{3,1,2,0:T(4,128)S(1)}, u32[]{:S(2)}, u32[]{:S(2)}) %collective-permute-start.23) | collective-permute-done | bytes 12320 | tf_op jit(solution)/shard_map/ppermute | solution.py:34
  347.2 4.3 collective-permute-start.24
  353.7 5.4 %collective-permute-start.26 = (f32[3,8,2,128]{3,1,2,0:T(8,128)S(1)}, f32[3,8,2,128]{3,1,2,0:T(8,128)S(1)}, u32[]{:S(2)}, u32[]{:S(2)}) collective-permute-start(f32[3,8,2,128]{3,1,2,0:T(8,128)S(1)} %get-tuple-element.487), channel_id=1, source_target_pairs={{0,1},{1,2},{2,3},{3,4},{4,5},{5,6},{6,7},{8,9},{9,10},{10,11},{11... | collective-permute-start | bytes 73736 | tf_op jit(solution)/shard_map/ppermute | solution.py:23
  361.1 43.7 %while.43 = (s32[]{:T(128)}, f32[3,8,20,132]{3,1,2,0:T(8,128)S(1)}, s32[16,4]{0,1:T(4,128)S(1)}, f32[16,3,4,4,4]{4,3,2,1,0:T(4,128)S(1)}, s32[]{:T(128)}) while((s32[]{:T(128)}, f32[3,8,20,132]{3,1,2,0:T(8,128)S(1)}, s32[16,4]{0,1:T(4,128)S(1)}, f32[16,3,4,4,4]{4,3,2,1,0:T(4,128)S(1)}, s32[]{:T(128)}) %tuple.219), condition=%wide.while_cond.19, body=%wide.while_body.19.sunk | while | flops 2 | bytes 50833 | solution.py:122
  407.7 10.8 %scatter_custom_fusion.3 = f32[3,21120]{0,1:T(8,128)} fusion(s32[1024]{0:T(1024)S(1)} %reshape.1316, f32[1024,3]{1,0:T(8,128)S(1)} %bitcast.208, f32[]{:T(128)} %constant.637.clone.1), kind=kCustom, calls=%fused_computation.20 | custom fusion | flops 3072 | bytes 253444
  418.4 6.4 %copy.76 = f32[3,21120]{1,0:T(4,128)S(1)} copy(f32[3,21120]{0,1:T(8,128)} %scatter_custom_fusion.3) | data formatting | bytes 506880
  425.7 3.1 collective-permute-start.28
  430.9 46.7 %all-reduce.4 = (f32[]{:T(128)}, f32[]{:T(128)}, f32[]{:T(128)}, f32[]{:T(128)}, f32[]{:T(128)}, /*index=5*/f32[]{:T(128)}, f32[]{:T(128)}, f32[]{:T(128)}) all-reduce(f32[]{:T(128)} %get-tuple-element.547, f32[]{:T(128)} %get-tuple-element.507, f32[]{:T(128)} %get-tuple-element.549, ...), channel_id=1, replica_groups=mesh['gx'=4,'gy'=8] {'gx','gy'}, use_global_device_ids=true, to_apply=%region_19.20 | all-reduce | flops 8 | bytes 64 | tf_op jit(solution)/shard_map/psum | solution.py:183
  485.6 4.3 collective-permute-start.30
  491.9 4.3 collective-permute-done.31
  (409 shorter events, 209.4 us)
Async XLA Ops:
  1.6 10.9 %collective-permute-start.1 = (f32[3,2,16,128]{3,1,2,0:T(2,128)S(1)}, f32[3,2,16,128]{3,1,2,0:T(2,128)S(1)}, u32[]{:S(2)}, u32[]{:S(2)}) collective-permute-start(f32[3,2,16,128]{3,1,2,0:T(2,128)S(1)} %get-tuple-element.526), channel_id=1, source_target_pairs={{8,0},{16,8},{24,16},{9,1},{17,9},{25,17},{10,2},{18,10},{26,18},{... | collective-permute-start | bytes 147464 | tf_op jit(solution)/shard_map/ppermute | solution.py:26
  2.9 9.6 %collective-permute-start = (f32[3,2,16,128]{3,1,2,0:T(2,128)S(1)}, f32[3,2,16,128]{3,1,2,0:T(2,128)S(1)}, u32[]{:S(2)}, u32[]{:S(2)}) collective-permute-start(f32[3,2,16,128]{3,1,2,0:T(2,128)S(1)} %get-tuple-element.525), channel_id=1, source_target_pairs={{0,8},{8,16},{16,24},{1,9},{9,17},{17,25},{2,10},{10,18},{18,26},{... | collective-permute-start | bytes 147464 | tf_op jit(solution)/shard_map/ppermute | solution.py:23
  12.5 49.5 %collective-permute-start.3 = (f32[3,8,2,128]{3,1,2,0:T(8,128)S(1)}, f32[3,8,2,128]{3,1,2,0:T(8,128)S(1)}, u32[]{:S(2)}, u32[]{:S(2)}) collective-permute-start(f32[3,8,2,128]{3,1,2,0:T(8,128)S(1)} %get-tuple-element.494), channel_id=1, source_target_pairs={{1,0},{2,1},{3,2},{4,3},{5,4},{6,5},{7,6},{9,8},{10,9},{11,10},{12... | collective-permute-start | bytes 73736 | tf_op jit(solution)/shard_map/ppermute | solution.py:26
  13.8 48.2 %collective-permute-start.2 = (f32[3,8,2,128]{3,1,2,0:T(8,128)S(1)}, f32[3,8,2,128]{3,1,2,0:T(8,128)S(1)}, u32[]{:S(2)}, u32[]{:S(2)}) collective-permute-start(f32[3,8,2,128]{3,1,2,0:T(8,128)S(1)} %get-tuple-element.493), channel_id=1, source_target_pairs={{0,1},{1,2},{2,3},{3,4},{4,5},{5,6},{6,7},{8,9},{9,10},{10,11},{11... | collective-permute-start | bytes 73736 | tf_op jit(solution)/shard_map/ppermute | solution.py:23
  109.8 34.0 %copy-start.1 = (f32[3,4,16,128]{3,2,1,0:T(8,128)S(1)}, f32[3,4,16,128]{3,2,1,0:T(8,128)}, u32[]{:S(2)}) copy-start(f32[3,4,16,128]{3,2,1,0:T(8,128)} %param.37) | copy-start | bytes 294916
  120.6 81.6 %copy-start = (f32[3,2048]{1,0:T(4,128)S(1)}, f32[3,2048]{1,0:T(4,128)}, u32[]{:S(2)}) copy-start(f32[3,2048]{1,0:T(4,128)} %param.39) | copy-start | bytes 73732
  127.9 3.0 collective-permute-start.4
  129.2 5.7 %collective-permute-start.5 = (f32[3,2,20,128]{3,1,2,0:T(2,128)S(1)}, f32[3,2,20,128]{3,1,2,0:T(2,128)S(1)}, u32[]{:S(2)}, u32[]{:S(2)}) collective-permute-start(f32[3,2,20,128]{3,1,2,0:T(2,128)S(1)} %get-tuple-element.485), channel_id=1, source_target_pairs={{8,0},{16,8},{24,16},{9,1},{17,9},{25,17},{10,2},{18,10},{26,18},{... | collective-permute-start | bytes 184328 | tf_op jit(solution)/shard_map/ppermute | solution.py:34
  134.9 4.6 collective-permute-start.6
  138.2 5.6 %collective-permute-start.7 = (f32[3,4,2,128]{3,1,2,0:T(4,128)S(1)}, f32[3,4,2,128]{3,1,2,0:T(4,128)S(1)}, u32[]{:S(2)}, u32[]{:S(2)}) collective-permute-start(f32[3,4,2,128]{3,1,2,0:T(4,128)S(1)} %get-tuple-element.517), channel_id=1, source_target_pairs={{1,0},{2,1},{3,2},{4,3},{5,4},{6,5},{7,6},{9,8},{10,9},{11,10},{12... | collective-permute-start | bytes 36872 | tf_op jit(solution)/shard_map/ppermute | solution.py:34
  144.0 5.3 %collective-permute-start.9 = (f32[3,2,16,128]{3,1,2,0:T(2,128)S(1)}, f32[3,2,16,128]{3,1,2,0:T(2,128)S(1)}, u32[]{:S(2)}, u32[]{:S(2)}) collective-permute-start(f32[3,2,16,128]{3,1,2,0:T(2,128)S(1)} %get-tuple-element.524), channel_id=1, source_target_pairs={{8,0},{16,8},{24,16},{9,1},{17,9},{25,17},{10,2},{18,10},{26,18},{... | collective-permute-start | bytes 147464 | tf_op jit(solution)/shard_map/ppermute | solution.py:26
  145.3 4.9 collective-permute-start.8
  150.2 6.0 %collective-permute-start.11 = (f32[3,8,2,128]{3,1,2,0:T(8,128)S(1)}, f32[3,8,2,128]{3,1,2,0:T(8,128)S(1)}, u32[]{:S(2)}, u32[]{:S(2)}) collective-permute-start(f32[3,8,2,128]{3,1,2,0:T(8,128)S(1)} %get-tuple-element.492), channel_id=1, source_target_pairs={{1,0},{2,1},{3,2},{4,3},{5,4},{6,5},{7,6},{9,8},{10,9},{11,10},{12... | collective-permute-start | bytes 73736 | tf_op jit(solution)/shard_map/ppermute | solution.py:26
  151.5 6.1 %collective-permute-start.10 = (f32[3,8,2,128]{3,1,2,0:T(8,128)S(1)}, f32[3,8,2,128]{3,1,2,0:T(8,128)S(1)}, u32[]{:S(2)}, u32[]{:S(2)}) collective-permute-start(f32[3,8,2,128]{3,1,2,0:T(8,128)S(1)} %get-tuple-element.491), channel_id=1, source_target_pairs={{0,1},{1,2},{2,3},{3,4},{4,5},{5,6},{6,7},{8,9},{9,10},{10,11},{11... | collective-permute-start | bytes 73736 | tf_op jit(solution)/shard_map/ppermute | solution.py:23
  222.6 4.7 collective-permute-start.12
  225.9 6.0 %collective-permute-start.13 = (f32[3,2,20,128]{3,1,2,0:T(2,128)S(1)}, f32[3,2,20,128]{3,1,2,0:T(2,128)S(1)}, u32[]{:S(2)}, u32[]{:S(2)}) collective-permute-start(f32[3,2,20,128]{3,1,2,0:T(2,128)S(1)} %get-tuple-element.483), channel_id=1, source_target_pairs={{8,0},{16,8},{24,16},{9,1},{17,9},{25,17},{10,2},{18,10},{26,18},{... | collective-permute-start | bytes 184328 | tf_op jit(solution)/shard_map/ppermute | solution.py:34
  232.0 6.7 %collective-permute-start.14 = (f32[3,4,2,128]{3,1,2,0:T(4,128)S(1)}, f32[3,4,2,128]{3,1,2,0:T(4,128)S(1)}, u32[]{:S(2)}, u32[]{:S(2)}) collective-permute-start(f32[3,4,2,128]{3,1,2,0:T(4,128)S(1)} %get-tuple-element.516), channel_id=1, source_target_pairs={{0,1},{1,2},{2,3},{3,4},{4,5},{5,6},{6,7},{8,9},{9,10},{10,11},{11... | collective-permute-start | bytes 36872 | tf_op jit(solution)/shard_map/ppermute | solution.py:34
  237.5 6.8 %collective-permute-start.15 = (f32[3,4,2,128]{3,1,2,0:T(4,128)S(1)}, f32[3,4,2,128]{3,1,2,0:T(4,128)S(1)}, u32[]{:S(2)}, u32[]{:S(2)}) collective-permute-start(f32[3,4,2,128]{3,1,2,0:T(4,128)S(1)} %get-tuple-element.515), channel_id=1, source_target_pairs={{1,0},{2,1},{3,2},{4,3},{5,4},{6,5},{7,6},{9,8},{10,9},{11,10},{12... | collective-permute-start | bytes 36872 | tf_op jit(solution)/shard_map/ppermute | solution.py:34
  244.5 5.6 %collective-permute-start.17 = (f32[3,2,16,128]{3,1,2,0:T(2,128)S(1)}, f32[3,2,16,128]{3,1,2,0:T(2,128)S(1)}, u32[]{:S(2)}, u32[]{:S(2)}) collective-permute-start(f32[3,2,16,128]{3,1,2,0:T(2,128)S(1)} %get-tuple-element.522), channel_id=1, source_target_pairs={{8,0},{16,8},{24,16},{9,1},{17,9},{25,17},{10,2},{18,10},{26,18},{... | collective-permute-start | bytes 147464 | tf_op jit(solution)/shard_map/ppermute | solution.py:26
  245.8 5.2 %collective-permute-start.16 = (f32[3,2,16,128]{3,1,2,0:T(2,128)S(1)}, f32[3,2,16,128]{3,1,2,0:T(2,128)S(1)}, u32[]{:S(2)}, u32[]{:S(2)}) collective-permute-start(f32[3,2,16,128]{3,1,2,0:T(2,128)S(1)} %get-tuple-element.521), channel_id=1, source_target_pairs={{0,8},{8,16},{16,24},{1,9},{9,17},{17,25},{2,10},{10,18},{18,26},{... | collective-permute-start | bytes 147464 | tf_op jit(solution)/shard_map/ppermute | solution.py:23
  250.9 6.7 %collective-permute-start.19 = (f32[3,8,2,128]{3,1,2,0:T(8,128)S(1)}, f32[3,8,2,128]{3,1,2,0:T(8,128)S(1)}, u32[]{:S(2)}, u32[]{:S(2)}) collective-permute-start(f32[3,8,2,128]{3,1,2,0:T(8,128)S(1)} %get-tuple-element.490), channel_id=1, source_target_pairs={{1,0},{2,1},{3,2},{4,3},{5,4},{6,5},{7,6},{9,8},{10,9},{11,10},{12... | collective-permute-start | bytes 73736 | tf_op jit(solution)/shard_map/ppermute | solution.py:26
  252.2 6.7 %collective-permute-start.18 = (f32[3,8,2,128]{3,1,2,0:T(8,128)S(1)}, f32[3,8,2,128]{3,1,2,0:T(8,128)S(1)}, u32[]{:S(2)}, u32[]{:S(2)}) collective-permute-start(f32[3,8,2,128]{3,1,2,0:T(8,128)S(1)} %get-tuple-element.489), channel_id=1, source_target_pairs={{0,1},{1,2},{2,3},{3,4},{4,5},{5,6},{6,7},{8,9},{9,10},{10,11},{11... | collective-permute-start | bytes 73736 | tf_op jit(solution)/shard_map/ppermute | solution.py:23
  323.9 4.8 collective-permute-start.20
  327.4 5.8 %collective-permute-start.21 = (f32[3,2,20,128]{3,1,2,0:T(2,128)S(1)}, f32[3,2,20,128]{3,1,2,0:T(2,128)S(1)}, u32[]{:S(2)}, u32[]{:S(2)}) collective-permute-start(f32[3,2,20,128]{3,1,2,0:T(2,128)S(1)} %get-tuple-element.481), channel_id=1, source_target_pairs={{8,0},{16,8},{24,16},{9,1},{17,9},{25,17},{10,2},{18,10},{26,18},{... | collective-permute-start | bytes 184328 | tf_op jit(solution)/shard_map/ppermute | solution.py:34
  333.4 6.8 %collective-permute-start.22 = (f32[3,4,2,128]{3,1,2,0:T(4,128)S(1)}, f32[3,4,2,128]{3,1,2,0:T(4,128)S(1)}, u32[]{:S(2)}, u32[]{:S(2)}) collective-permute-start(f32[3,4,2,128]{3,1,2,0:T(4,128)S(1)} %get-tuple-element.514), channel_id=1, source_target_pairs={{0,1},{1,2},{2,3},{3,4},{4,5},{5,6},{6,7},{8,9},{9,10},{10,11},{11... | collective-permute-start | bytes 36872 | tf_op jit(solution)/shard_map/ppermute | solution.py:34
  338.9 6.8 %collective-permute-start.23 = (f32[3,4,2,128]{3,1,2,0:T(4,128)S(1)}, f32[3,4,2,128]{3,1,2,0:T(4,128)S(1)}, u32[]{:S(2)}, u32[]{:S(2)}) collective-permute-start(f32[3,4,2,128]{3,1,2,0:T(4,128)S(1)} %get-tuple-element.513), channel_id=1, source_target_pairs={{1,0},{2,1},{3,2},{4,3},{5,4},{6,5},{7,6},{9,8},{10,9},{11,10},{12... | collective-permute-start | bytes 36872 | tf_op jit(solution)/shard_map/ppermute | solution.py:34
  345.9 5.6 %collective-permute-start.25 = (f32[3,2,16,128]{3,1,2,0:T(2,128)S(1)}, f32[3,2,16,128]{3,1,2,0:T(2,128)S(1)}, u32[]{:S(2)}, u32[]{:S(2)}) collective-permute-start(f32[3,2,16,128]{3,1,2,0:T(2,128)S(1)} %get-tuple-element.520), channel_id=1, source_target_pairs={{8,0},{16,8},{24,16},{9,1},{17,9},{25,17},{10,2},{18,10},{26,18},{... | collective-permute-start | bytes 147464 | tf_op jit(solution)/shard_map/ppermute | solution.py:26
  347.2 5.2 %collective-permute-start.24 = (f32[3,2,16,128]{3,1,2,0:T(2,128)S(1)}, f32[3,2,16,128]{3,1,2,0:T(2,128)S(1)}, u32[]{:S(2)}, u32[]{:S(2)}) collective-permute-start(f32[3,2,16,128]{3,1,2,0:T(2,128)S(1)} %get-tuple-element.519), channel_id=1, source_target_pairs={{0,8},{8,16},{16,24},{1,9},{9,17},{17,25},{2,10},{10,18},{18,26},{... | collective-permute-start | bytes 147464 | tf_op jit(solution)/shard_map/ppermute | solution.py:23
  352.4 6.7 %collective-permute-start.27 = (f32[3,8,2,128]{3,1,2,0:T(8,128)S(1)}, f32[3,8,2,128]{3,1,2,0:T(8,128)S(1)}, u32[]{:S(2)}, u32[]{:S(2)}) collective-permute-start(f32[3,8,2,128]{3,1,2,0:T(8,128)S(1)} %get-tuple-element.488), channel_id=1, source_target_pairs={{1,0},{2,1},{3,2},{4,3},{5,4},{6,5},{7,6},{9,8},{10,9},{11,10},{12... | collective-permute-start | bytes 73736 | tf_op jit(solution)/shard_map/ppermute | solution.py:26
  353.7 6.7 %collective-permute-start.26 = (f32[3,8,2,128]{3,1,2,0:T(8,128)S(1)}, f32[3,8,2,128]{3,1,2,0:T(8,128)S(1)}, u32[]{:S(2)}, u32[]{:S(2)}) collective-permute-start(f32[3,8,2,128]{3,1,2,0:T(8,128)S(1)} %get-tuple-element.487), channel_id=1, source_target_pairs={{0,1},{1,2},{2,3},{3,4},{4,5},{5,6},{6,7},{8,9},{9,10},{10,11},{11... | collective-permute-start | bytes 73736 | tf_op jit(solution)/shard_map/ppermute | solution.py:23
  425.7 59.7 %collective-permute-start.28 = (f32[3,2,20,128]{3,1,2,0:T(2,128)S(1)}, f32[3,2,20,128]{3,1,2,0:T(2,128)S(1)}, u32[]{:S(2)}, u32[]{:S(2)}) collective-permute-start(f32[3,2,20,128]{3,1,2,0:T(2,128)S(1)} %get-tuple-element.480), channel_id=1, source_target_pairs={{0,8},{8,16},{16,24},{1,9},{9,17},{17,25},{2,10},{10,18},{18,26},{... | collective-permute-start | bytes 184328 | tf_op jit(solution)/shard_map/ppermute | solution.py:34
  429.6 55.9 %collective-permute-start.29 = (f32[3,2,20,128]{3,1,2,0:T(2,128)S(1)}, f32[3,2,20,128]{3,1,2,0:T(2,128)S(1)}, u32[]{:S(2)}, u32[]{:S(2)}) collective-permute-start(f32[3,2,20,128]{3,1,2,0:T(2,128)S(1)} %get-tuple-element.479), channel_id=1, source_target_pairs={{8,0},{16,8},{24,16},{9,1},{17,9},{25,17},{10,2},{18,10},{26,18},{... | collective-permute-start | bytes 184328 | tf_op jit(solution)/shard_map/ppermute | solution.py:34
  485.6 6.2 %collective-permute-start.30 = (f32[3,4,2,128]{3,1,2,0:T(4,128)S(1)}, f32[3,4,2,128]{3,1,2,0:T(4,128)S(1)}, u32[]{:S(2)}, u32[]{:S(2)}) collective-permute-start(f32[3,4,2,128]{3,1,2,0:T(4,128)S(1)} %get-tuple-element.512), channel_id=1, source_target_pairs={{0,1},{1,2},{2,3},{3,4},{4,5},{5,6},{6,7},{8,9},{9,10},{10,11},{11... | collective-permute-start | bytes 36872 | tf_op jit(solution)/shard_map/ppermute | solution.py:34
  490.6 5.6 %collective-permute-start.31 = (f32[3,4,2,128]{3,1,2,0:T(4,128)S(1)}, f32[3,4,2,128]{3,1,2,0:T(4,128)S(1)}, u32[]{:S(2)}, u32[]{:S(2)}) collective-permute-start(f32[3,4,2,128]{3,1,2,0:T(4,128)S(1)} %get-tuple-element.511), channel_id=1, source_target_pairs={{1,0},{2,1},{3,2},{4,3},{5,4},{6,5},{7,6},{9,8},{10,9},{11,10},{12... | collective-permute-start | bytes 36872 | tf_op jit(solution)/shard_map/ppermute | solution.py:34
where the time goes:
time: 500 us; the launch traced here: 497 us
  local copies, waits for them, and re-layouts  209 us (42%)
  blocking collectives  88.7 us (18%)
  starting transfers between devices  84 us (17%)
  other arithmetic  55.9 us (11%)
  waiting for transfers between devices  38.5 us (8%)
  between operations  10.7 us (2%)
  matrix products  9.2 us (2%)
    gather x256, local copies, waits for them, and re-layouts  174 us
    psum x1, blocking collectives, shards(): summed = lax.psum((data_sq, spread), ('gx', 'gy'))  46.7 us
    unnamed x7, other arithmetic  44.6 us
    psum x1, blocking collectives, shards(): lax.psum(jnp.sum(block_fill).astype(jnp.float32), ('gx', 'gy'))  42 us
    ppermute x16, starting transfers between devices, shifted(): return lax.ppermute(value, axis, pairs)  37.1 us
    ppermute x8, starting transfers between devices, with_halo(): lax.ppermute(lax.slice_in_dim(block, block.shape[dim] - width, None, axis...  36.6 us
    ppermute x16, waiting for transfers between devices, shifted(): return lax.ppermute(value, axis, pairs)  32.1 us
    unnamed x19, local copies, waits for them, and re-layouts  30.1 us
  transfers between devices with their start and end apart: 32, of which 13 were waited for; matrix products, arithmetic and copies ran while one was open for 2% of the time, Pallas kernels for 0%

commit v1 on v0

v1 whole, which is shorter than its diff:
```python
import functools

import jax
import jax.numpy as jnp
from jax import lax
from jax.experimental import pallas as pl
from jax.experimental.pallas import tpu as pltpu
from jax.sharding import PartitionSpec as P

ITERS = 4

penalty_weight = 0.5
learn_rate = 0.05
beta_one = 0.9
beta_two = 0.999
adam_eps = 0.1

MESH = pl.DeviceIdType.MESH
DIRS = ((1, 0), (-1, 0), (0, 1), (0, -1), (1, 1), (-1, 1), (1, -1), (-1, -1))
F32 = jnp.float32
BF16 = jnp.bfloat16


def cubic(u):
    one = 1.0 - u
    return (
        one * one * one / 6.0,
        (3.0 * u * u * u - 6.0 * u * u + 4.0) / 6.0,
        (-3.0 * u * u * u + 3.0 * u * u + 3.0 * u + 1.0) / 6.0,
        u * u * u / 6.0,
    )


def split(x):
    hi = x.astype(BF16)
    lo = (x - hi.astype(F32)).astype(BF16)
    return hi, lo


def mm(a, b):
    return jnp.dot(a, b, preferred_element_type=F32)


def mm_nt(a, b):
    return lax.dot_general(a, b, (((1,), (1,)), ((), ())), preferred_element_type=F32)


def iota(shape, dim):
    return lax.broadcasted_iota(jnp.int32, shape, dim)


def kernel(
    nx, ny, cell_ref, fill_ref, coef_ref, frac_ref, targ_ref, out_ref, loss_ref,
    cur, mom, sec, grad, total, wt_hi, wt_lo, uv, sel, sel_t, term, sy, sc, rx, ry, rc,
    red_src, red_x, red_y, send_sem, recv_sem, rs_x, rr_x, rs_y, rr_y,
):
    comps, cx, cy, nz = coef_ref.shape
    blocks = cell_ref.shape[0]
    ex, ey = cx + 3, cy + 8
    rows = ex * ey
    gx, gy = lax.axis_index("gx"), lax.axis_index("gy")
    ncells = float(cx * nx * cy * ny * nz)
    low_rows = (ey - 1, 0, 1)
    high_rows = (cy - 1, cy, cy + 1)

    def here(d, sign):
        x, y = gx + sign * d[0], gy + sign * d[1]
        return (x >= 0) & (x < nx) & (y >= 0) & (y < ny)

    can_send = [here(d, 1) for d in DIRS]
    can_recv = [here(d, -1) for d in DIRS]

    barrier = pltpu.get_barrier_semaphore()
    for n, d in enumerate(DIRS):
        @pl.when(can_send[n])
        def _():
            pl.semaphore_signal(barrier, inc=1, device_id=(gx + d[0], gy + d[1]), device_id_type=MESH)
    for k in range(1, nx):
        pl.semaphore_signal(barrier, inc=1, device_id=(lax.rem(gx + k, nx), gy), device_id_type=MESH)
    for k in range(1, ny):
        pl.semaphore_signal(barrier, inc=1, device_id=(gx, lax.rem(gy + k, ny)), device_id_type=MESH)

    def reduce_copy(kind, stage, k):
        if stage == 0:
            return pltpu.make_async_remote_copy(
                src_ref=red_src.at[kind, 0], dst_ref=red_x.at[kind, k - 1],
                send_sem=rs_x.at[kind, k - 1], recv_sem=rr_x.at[kind, k - 1],
                device_id=(lax.rem(gx + k, nx), gy), device_id_type=MESH)
        return pltpu.make_async_remote_copy(
            src_ref=red_src.at[kind, 1], dst_ref=red_y.at[kind, k - 1],
            send_sem=rs_y.at[kind, k - 1], recv_sem=rr_y.at[kind, k - 1],
            device_id=(gx, lax.rem(gy + k, ny)), device_id_type=MESH)

    def reduce_start(kind, stage, value):
        red_src[kind, stage] = value
        for k in range(1, ny if stage else nx):
            reduce_copy(kind, stage, k).start()

    def reduce_wait(kind, stage):
        value = red_src[kind, stage]
        for k in range(1, ny if stage else nx):
            reduce_copy(kind, stage, k).wait_recv()
            value = value + (red_y if stage else red_x)[kind, k - 1]
        for k in range(1, ny if stage else nx):
            reduce_copy(kind, stage, k).wait_send()
        return value

    def face_copy(n, slot):
        d = DIRS[n]
        if n < 2:
            src = grad.at[:, pl.ds(cx if n == 0 else 0, 3)]
            dst = rx.at[slot, n]
        elif n < 4:
            src, dst = sy.at[n - 2], ry.at[slot, n - 2]
        else:
            src, dst = sc.at[n - 4], rc.at[slot, n - 4]
        return pltpu.make_async_remote_copy(
            src_ref=src, dst_ref=dst, send_sem=send_sem.at[slot, n], recv_sem=recv_sem.at[slot, n],
            device_id=(gx + d[0], gy + d[1]), device_id_type=MESH)

    sub = iota((8, nz), 0)

    def send_faces(slot):
        for n in range(2):
            @pl.when(can_send[n])
            def _():
                face_copy(n, slot).start()
        for side in range(2):
            tiles = []
            for c in range(comps):
                for k in range(3):
                    row = (high_rows, low_rows)[side][k]
                    tile = jnp.concatenate(
                        [grad[c, x, row : row + 1, :] for x in range(ex)]
                        + [jnp.zeros((8 - ex, nz), F32)], axis=0)
                    sy[side, 3 * c + k] = tile
                    tiles.append(tile)
            turned = [pltpu.roll(t, 4, 0) for t in tiles]
            for j in range(5):
                late = min(j + 5, 8)
                sc[2 * side, j] = jnp.where(sub < 4, turned[j], tiles[late])
                sc[2 * side + 1, j] = jnp.where(sub < 4, tiles[j], turned[late])
        for n in range(2, 8):
            @pl.when(can_send[n])
            def _():
                face_copy(n, slot).start()

    def recv_faces(slot):
        for n in range(8):
            @pl.when(can_recv[n])
            def _():
                face_copy(n, slot).wait_recv()
        for c in range(comps):
            for x in range(ex):
                value = grad[c, x]
                if x < 3:
                    value = value + rx[slot, 0, c, x]
                if x >= cx:
                    value = value + rx[slot, 1, c, x - cx]
                total[c, x] = value
        for side in range(2):
            for q in range(3 * comps):
                c, k = q // 3, q % 3
                row = (low_rows, high_rows)[side][k]
                below = rc[slot, 2 * side, q] if q < 5 else pltpu.roll(rc[slot, 2 * side, q - 5], 4, 0)
                above = pltpu.roll(rc[slot, 2 * side + 1, q], 4, 0) if q < 5 else rc[slot, 2 * side + 1, q - 5]
                tile = ry[slot, side, q] + jnp.where(sub < 3, below, jnp.where(sub > 3, above, 0.0))
                for x in range(ex):
                    total[c, x, row : row + 1, :] = total[c, x, row : row + 1, :] + tile[x : x + 1]

    def wait_sends(slot):
        for n in range(8):
            @pl.when(can_send[n])
            def _():
                face_copy(n, slot).wait_send()

    grad[...] = jnp.zeros_like(grad)
    grad[:, 1 : cx + 1, 0:cy, :] = coef_ref[...]
    mom[...] = jnp.zeros_like(mom)
    sec[...] = jnp.zeros_like(sec)
    for n in range(8):
        @pl.when(jnp.logical_not(can_recv[n]))
        def _():
            if n < 2:
                rx[:, n] = jnp.zeros((ITERS + 1, comps, 3, ey, nz), F32)
            elif n < 4:
                ry[:, n - 2] = jnp.zeros((ITERS + 1, 3 * comps, 8, nz), F32)
            else:
                rc[:, n - 4] = jnp.zeros((ITERS + 1, 5, 8, nz), F32)

    live = jnp.int32(0)
    for b in range(blocks):
        live = live + fill_ref[b]

    expected = jnp.int32(nx + ny - 2)
    for n in range(8):
        expected = expected + can_send[n].astype(jnp.int32)
    pl.semaphore_wait(barrier, expected)

    reduce_start(0, 0, jnp.full((8, nz), live, jnp.int32).astype(F32))
    send_faces(0)

    lane_b = iota((8, 16 * blocks), 1) // 16
    target = jnp.zeros((8, 16 * blocks), jnp.int32)
    ab_lane = iota((8, 16 * blocks), 1) % 16
    base_x = jnp.zeros((8, 16 * blocks), jnp.int32)
    base_y = jnp.zeros((8, 16 * blocks), jnp.int32)
    s_ab = iota((16, rows), 0)
    s_row = iota((16, rows), 1)
    zz = iota((nz, 128), 0)
    for b in range(blocks):
        cell = cell_ref[b]
        lx, ly, lz = cell // (cy * nz), cell // nz % cy, cell % nz
        base_x = jnp.where(lane_b == b, lx, base_x)
        base_y = jnp.where(lane_b == b, ly, base_y)
        y = ly - 1 + s_ab % 4
        y = jnp.where(y < 0, y + ey, y)
        sel_t[16 * b : 16 * (b + 1), :] = ((lx + s_ab // 4) * ey + y == s_row).astype(F32).astype(BF16)
        f = [frac_ref[c : c + 1, 128 * b : 128 * (b + 1)] for c in range(3)]
        bu, bv, bw = cubic(f[0]), cubic(f[1]), cubic(f[2])
        uv[b] = jnp.concatenate([bu[i] * bv[j] for i in range(4) for j in range(4)], axis=0)
        place = zz - (lz - 1)
        w = jnp.zeros((nz, 128), F32)
        for e in range(4):
            w = jnp.where(place == e, bw[e], w)
        wt_hi[b], wt_lo[b] = split(w)
    y = base_y - 1 + ab_lane % 4
    y = jnp.where(y < 0, y + ey, y)
    target = ((base_x + ab_lane // 4) * ey + y)[0:1]
    sel[...] = (iota((rows, 16 * blocks), 0) == target).astype(F32).astype(BF16)

    reduce_start(0, 1, reduce_wait(0, 0))
    recv_faces(0)
    cur[...] = total[...]
    wait_sends(0)
    grand = reduce_wait(0, 1)
    scale = (ncells / grand)[0:1]
    lane = iota((ey, nz), 1)
    y_row = iota((ey, nz), 0)
    own_y = y_row < cy
    top, bottom = gy == ny - 1, gy == 0
    mask_y = jnp.where(
        own_y, 1.0,
        jnp.where(y_row < cy + 2, jnp.where(top, 0.0, 1.0), jnp.where(bottom, 0.0, 1.0)),
    )
    mask_x = [None] * ex
    mask_x[0] = jnp.where(gx == 0, 0.0, 1.0)
    for x in range(cx + 1, ex):
        mask_x[x] = jnp.where(gx == nx - 1, 0.0, 1.0)

    def up_y(v):
        return pltpu.roll(v, ey - 1, 0)

    def down_y(v):
        return pltpu.roll(v, 1, 0)

    def up_z(v):
        return jnp.where(lane == nz - 1, 0.0, pltpu.roll(v, nz - 1, 1))

    def down_z(v):
        return jnp.where(lane == 0, 0.0, pltpu.roll(v, 1, 1))

    def forward(slot):
        parts = [split(cur[c].reshape(rows, nz)) for c in range(comps)]
        stack = jnp.concatenate([p[0] for p in parts] + [p[1] for p in parts], axis=1)
        picked = mm(sel_t[...], stack).astype(BF16)
        data = jnp.zeros((1, 128), F32)
        for b in range(blocks):
            r = slice(16 * b, 16 * (b + 1))
            hi = jnp.concatenate([picked[r, nz * c : nz * (c + 1)] for c in range(comps)], axis=0)
            lo = jnp.concatenate([picked[r, nz * (comps + c) : nz * (comps + c + 1)] for c in range(comps)], axis=0)
            whi, wlo = wt_hi[b], wt_lo[b]
            q = mm(hi, whi) + mm(lo, whi) + mm(hi, wlo)
            u = uv[b]
            alive = iota((1, 128), 1) < fill_ref[b]
            back = []
            for c in range(comps):
                v = jnp.sum(q[16 * c : 16 * (c + 1)] * u, axis=0, keepdims=True)
                mis = jnp.where(alive, v - targ_ref[c : c + 1, 128 * b : 128 * (b + 1)], 0.0)
                data = data + mis * mis
                back.append((mis * (2.0 * scale)) * u)
            dhi, dlo = split(jnp.concatenate(back, axis=0))
            t = mm_nt(dhi, whi) + mm_nt(dlo, whi) + mm_nt(dhi, wlo)
            thi, tlo = split(t)
            for c in range(comps):
                term[r, nz * c : nz * (c + 1)] = thi[16 * c : 16 * (c + 1)]
                term[r, nz * (comps + c) : nz * (comps + c + 1)] = tlo[16 * c : 16 * (c + 1)]
        pulled = mm(sel[...], term[...])
        spread = jnp.zeros((ey, nz), F32)
        div = []
        for x in range(1, cx + 1):
            one, two = cur[1, x], cur[2, x]
            dv = (cur[0, x + 1] - cur[0, x - 1] + up_y(one) - down_y(one) + up_z(two) - down_z(two)) / 2.0
            dv = jnp.where(own_y, dv, 0.0)
            spread = spread + dv * dv
            div.append(dv)
        for c in range(comps):
            whole = pulled[:, nz * c : nz * (c + 1)] + pulled[:, nz * (comps + c) : nz * (comps + c + 1)]
            for x in range(ex):
                value = whole[ey * x : ey * (x + 1)]
                if c == 0:
                    if 0 <= x - 2 < cx:
                        value = value + penalty_weight * div[x - 2]
                    if x < cx:
                        value = value - penalty_weight * div[x]
                elif 1 <= x <= cx:
                    dv = div[x - 1]
                    if c == 1:
                        value = value + penalty_weight * (down_y(dv) - up_y(dv))
                    else:
                        value = value + penalty_weight * (down_z(dv) - up_z(dv))
                grad[c, x] = value
        return data * (scale / ncells) + (penalty_weight / ncells) * jnp.sum(spread, axis=0, keepdims=True)

    def update(step):
        def pick(values):
            out = jnp.float32(values[-1])
            for i in range(ITERS - 1):
                out = jnp.where(step == i, jnp.float32(values[i]), out)
            return out
        rate = pick([learn_rate / (1.0 - beta_one ** (i + 1)) for i in range(ITERS)])
        corr = pick([1.0 / (1.0 - beta_two ** (i + 1)) for i in range(ITERS)])
        for c in range(comps):
            for x in range(ex):
                g = total[c, x] * mask_y
                if mask_x[x] is not None:
                    g = g * mask_x[x]
                m = beta_one * mom[c, x] + (1.0 - beta_one) * g
                s = beta_two * sec[c, x] + (1.0 - beta_two) * g * g
                mom[c, x], sec[c, x] = m, s
                cur[c, x] = cur[c, x] - (rate * m) / (jnp.sqrt(s * corr) + adam_eps)

    def body(step, losses):
        loss = forward(step)
        losses = jnp.where(sub == step, loss, losses)
        send_faces(step + 1)

        @pl.when(step == ITERS - 1)
        def _():
            reduce_start(1, 0, losses)

        recv_faces(step + 1)

        @pl.when(step == ITERS - 1)
        def _():
            reduce_start(1, 1, reduce_wait(1, 0))

        update(step)
        wait_sends(step + 1)
        return losses

    lax.fori_loop(0, ITERS, body, jnp.zeros((8, nz), F32))
    out_ref[...] = cur[:, 1 : cx + 1, 0:cy, :]
    final = reduce_wait(1, 1)
    for i in range(ITERS):
        loss_ref[i] = jnp.sum(final[i : i + 1])


def shards(nx, ny, coefficients, fractions, targets, block_cell, block_fill):
    comps, cx, cy, nz = coefficients.shape
    blocks = block_cell.shape[0]
    ex, ey = cx + 3, cy + 8
    rows = ex * ey
    state = pltpu.VMEM((comps, ex, ey, nz), F32)
    smem = pl.BlockSpec(memory_space=pltpu.SMEM)
    vmem = pl.BlockSpec(memory_space=pltpu.VMEM)
    dma = pltpu.SemaphoreType.DMA
    slots = ITERS + 1
    return pl.pallas_call(
        functools.partial(kernel, nx, ny),
        out_shape=(
            jax.ShapeDtypeStruct(coefficients.shape, F32),
            jax.ShapeDtypeStruct((ITERS,), F32),
        ),
        in_specs=[smem, smem, vmem, vmem, vmem],
        out_specs=(vmem, smem),
        scratch_shapes=[
            state, state, state, state, state,
            pltpu.VMEM((blocks, nz, 128), BF16),
            pltpu.VMEM((blocks, nz, 128), BF16),
            pltpu.VMEM((blocks, 16, 128), F32),
            pltpu.VMEM((rows, 16 * blocks), BF16),
            pltpu.VMEM((16 * blocks, rows), BF16),
            pltpu.VMEM((16 * blocks, 2 * comps * nz), BF16),
            pltpu.VMEM((2, 3 * comps, 8, nz), F32),
            pltpu.VMEM((4, 5, 8, nz), F32),
            pltpu.VMEM((slots, 2, comps, 3, ey, nz), F32),
            pltpu.VMEM((slots, 2, 3 * comps, 8, nz), F32),
            pltpu.VMEM((slots, 4, 5, 8, nz), F32),
            pltpu.VMEM((2, 2, 8, nz), F32),
            pltpu.VMEM((2, nx - 1, 8, nz), F32),
            pltpu.VMEM((2, ny - 1, 8, nz), F32),
            dma((slots, 8)), dma((slots, 8)),
            dma((2, nx - 1)), dma((2, nx - 1)),
            dma((2, ny - 1)), dma((2, ny - 1)),
        ],
        compiler_params=pltpu.CompilerParams(
            collective_id=0, has_side_effects=True, vmem_limit_bytes=32 * 1024 * 1024
        ),
    )(block_cell, block_fill, coefficients, fractions, targets)


def solution(mesh):
    nx, ny = mesh.shape["gx"], mesh.shape["gy"]
    return jax.shard_map(
        functools.partial(shards, nx, ny),
        mesh=mesh,
        in_specs=(
            P(None, "gx", "gy", None),
            P(None, ("gx", "gy")),
            P(None, ("gx", "gy")),
            P(("gx", "gy")),
            P(("gx", "gy")),
        ),
        out_specs=(P(None, "gx", "gy", None), P()),
        check_vma=False,
    )
```

time: 500 us -> 53.8 us (0.11)
  local copies, waits for them, and re-layouts: 209 us -> 4.86 us
  blocking collectives: 88.7 us -> 0 us
  starting transfers between devices: 84 us -> 0 us
  other arithmetic: 55.9 us -> 0 us
  Pallas kernels: 0 us -> 48 us
  waiting for transfers between devices: 38.5 us -> 0 us
  between operations: 10.7 us -> 0.65 us
  matrix products: 9.2 us -> 0 us
    gather x260 -> x0, local copies, waits for them, and re-layouts: 175 us -> none
    psum x2 -> x0, blocking collectives: 88.7 us -> none  [the longest x1 46.7 us: shards(): summed = lax.psum((data_sq, spread), ('gx', 'gy'))]
    ppermute x32 -> x0, starting transfers between devices: 84 us -> none  [the longest x16 37.1 us: shifted(): return lax.ppermute(value, axis, pairs)]
    pallas_call x0 -> x1, Pallas kernels: none -> 48 us  [shards(): pl.pallas_call(functools.partial(kernel, nx, ny), out_shape=(jax.ShapeDty...]
    unnamed x7 -> x0, other arithmetic: 44.6 us -> none
    ppermute x32 -> x0, waiting for transfers between devices: 38.5 us -> none  [the longest x16 32.1 us: shifted(): return lax.ppermute(value, axis, pairs)]
    unnamed x19 -> x12, local copies, waits for them, and re-layouts: 30.1 us -> 4.86 us
    dot_general x8 -> x0, matrix products: 9.2 us -> none  [the longest x4 5.5 us: one_round(): jnp.einsum('gsn,gcn->cgs', basis_mat, patches, precision=lax.Precision.HI...]
  transfers between devices with their start and end apart: 32 -> 0, of which waited for: 13 -> 0; matrix products, arithmetic and copies ran while one was open for 2% -> 0% of each run, Pallas kernels for 0% -> 0%
where the time goes in v1:
time: 53.8 us; the launch traced here: 53.5 us
  Pallas kernels  48 us (89%)
  local copies, waits for them, and re-layouts  4.86 us (9%)
  between operations  0.65 us (1%)
    pallas_call x1, Pallas kernels, shards(): pl.pallas_call(functools.partial(kernel, nx, ny), out_shape=(jax.ShapeDty...  48 us
    unnamed x12, local copies, waits for them, and re-layouts  4.86 us

profile of v1, /device:TPU:0, one launch (start us, length us, event | category | flops | bytes accessed | tf_op | source)
XLA Modules:
  0.0 53.5 jit_solution(6783495362057300321)
XLA Ops:
  0.6 0.0 copy-start
  0.6 0.9 %copy-done = f32[3,4,16,128]{3,2,1,0:T(8,128)S(1)} copy-done((f32[3,4,16,128]{3,2,1,0:T(8,128)S(1)}, f32[3,4,16,128]{3,2,1,0:T(8,128)}, u32[]{:S(2)}) %copy-start) | copy-done | bytes 98328
  1.5 0.0 copy-start.1
  1.5 0.8 %copy-done.1 = f32[3,2048]{1,0:T(4,128)S(1)} copy-done((f32[3,2048]{1,0:T(4,128)S(1)}, f32[3,2048]{1,0:T(4,128)}, u32[]{:S(2)}) %copy-start.1) | copy-done | bytes 24600
  2.3 0.0 copy-start.2
  2.3 0.8 %copy-done.2 = f32[3,2048]{1,0:T(4,128)S(1)} copy-done((f32[3,2048]{1,0:T(4,128)S(1)}, f32[3,2048]{1,0:T(4,128)}, u32[]{:S(2)}) %copy-start.2) | copy-done | bytes 24600
  3.0 0.0 copy-start.3
  3.0 0.7 %copy-done.3 = s32[16]{0:T(128)S(1)} copy-done((s32[16]{0:T(128)S(1)}, s32[16]{0:T(128)}, u32[]{:S(2)}) %copy-start.3) | copy-done | bytes 88
  3.7 0.0 copy-start.4
  3.7 0.7 %copy-done.4 = s32[16]{0:T(128)S(1)} copy-done((s32[16]{0:T(128)S(1)}, s32[16]{0:T(128)}, u32[]{:S(2)}) %copy-start.4) | copy-done | bytes 88
  4.4 48.0 %shard_map.68 = (f32[3,4,16,128]{3,2,1,0:T(8,128)S(1)}, f32[4]{0:T(128)S(1)}) custom-call(s32[16]{0:T(128)S(1)} %copy-done.3, s32[16]{0:T(128)S(1)} %copy-done.4, f32[3,4,16,128]{3,2,1,0:T(8,128)S(1)} %copy-done, f32[3,2048]{1,0:T(4,128)S(1)} %copy-done.1, f32[3,2048]{1,0:T(4,128)S(1)} %copy-done.2), custom_call_target="tpu_custom_call" | custom-call | tf_op jit(solution)/shard_map/pallas_call | solution.py:369
  52.4 0.6 %copy.9 = f32[3,4,16,128]{3,2,1,0:T(8,128)} copy(f32[3,4,16,128]{3,2,1,0:T(8,128)S(1)} %get-tuple-element.4) | data formatting | bytes 196608
  53.0 0.5 copy.10
Async XLA Ops:
  0.6 0.9 %copy-start = (f32[3,4,16,128]{3,2,1,0:T(8,128)S(1)}, f32[3,4,16,128]{3,2,1,0:T(8,128)}, u32[]{:S(2)}) copy-start(f32[3,4,16,128]{3,2,1,0:T(8,128)} %coef_ref.1) | copy-start | bytes 294916
  1.5 0.8 %copy-start.1 = (f32[3,2048]{1,0:T(4,128)S(1)}, f32[3,2048]{1,0:T(4,128)}, u32[]{:S(2)}) copy-start(f32[3,2048]{1,0:T(4,128)} %frac_ref.1) | copy-start | bytes 73732
  2.3 0.8 %copy-start.2 = (f32[3,2048]{1,0:T(4,128)S(1)}, f32[3,2048]{1,0:T(4,128)}, u32[]{:S(2)}) copy-start(f32[3,2048]{1,0:T(4,128)} %targ_ref.1) | copy-start | bytes 73732
  3.0 0.7 %copy-start.3 = (s32[16]{0:T(128)S(1)}, s32[16]{0:T(128)}, u32[]{:S(2)}) copy-start(s32[16]{0:T(128)} %cell_ref.1) | copy-start | bytes 196
  3.7 0.7 %copy-start.4 = (s32[16]{0:T(128)S(1)}, s32[16]{0:T(128)}, u32[]{:S(2)}) copy-start(s32[16]{0:T(128)} %fill_ref.1) | copy-start | bytes 196

commit v2 on v1

--- a/solution.py
+++ b/solution.py
@@ -41,8 +41,10 @@
     return jnp.dot(a, b, preferred_element_type=F32)
 
 
-def mm_nt(a, b):
-    return lax.dot_general(a, b, (((1,), (1,)), ((), ())), preferred_element_type=F32)
+def folded(hi, lo, w):
+    both = mm(jnp.concatenate([hi, lo], axis=1), w)
+    half = both.shape[1] // 2
+    return both[:, :half] + both[:, half:]
 
 
 def iota(shape, dim):
@@ -50,10 +52,19 @@
 
 
 def kernel(
-    nx, ny, cell_ref, fill_ref, coef_ref, frac_ref, targ_ref, out_ref, loss_ref,
-    cur, mom, sec, grad, total, wt_hi, wt_lo, uv, sel, sel_t, term, sy, sc, rx, ry, rc,
+    nx, ny, cell_in, fill_in, coef_in, frac_in, targ_in, out_ref, loss_ref,
+    cell_ref, fill_ref, coef_ref, frac_ref, targ_ref, in_sem,
+    cur, mom, sec, grad, total, w_ahead, w_back, uv, sel, sel_t, term, sy, sc, rx, ry, rc,
     red_src, red_x, red_y, send_sem, recv_sem, rs_x, rr_x, rs_y, rr_y,
 ):
+    loads = [
+        pltpu.make_async_copy(src, dst, in_sem.at[n])
+        for n, (src, dst) in enumerate((
+            (coef_in, coef_ref), (fill_in, fill_ref), (cell_in, cell_ref),
+            (frac_in, frac_ref), (targ_in, targ_ref)))
+    ]
+    for load in loads:
+        load.start()
     comps, cx, cy, nz = coef_ref.shape
     blocks = cell_ref.shape[0]
     ex, ey = cx + 3, cy + 8
@@ -175,7 +186,6 @@
                 face_copy(n, slot).wait_send()
 
     grad[...] = jnp.zeros_like(grad)
-    grad[:, 1 : cx + 1, 0:cy, :] = coef_ref[...]
     mom[...] = jnp.zeros_like(mom)
     sec[...] = jnp.zeros_like(sec)
     for n in range(8):
@@ -188,6 +198,9 @@
             else:
                 rc[:, n - 4] = jnp.zeros((ITERS + 1, 5, 8, nz), F32)
 
+    for load in loads:
+        load.wait()
+    grad[:, 1 : cx + 1, 0:cy, :] = coef_ref[...]
     live = jnp.int32(0)
     for b in range(blocks):
         live = live + fill_ref[b]
@@ -223,7 +236,10 @@
         w = jnp.zeros((nz, 128), F32)
         for e in range(4):
             w = jnp.where(place == e, bw[e], w)
-        wt_hi[b], wt_lo[b] = split(w)
+        for mat, ref in ((w, w_ahead), (w.T, w_back)):
+            hi, lo = split(mat)
+            ref[b] = jnp.concatenate(
+                [jnp.concatenate([hi, lo], axis=1), jnp.concatenate([hi, jnp.zeros_like(lo)], axis=1)], axis=0)
     y = base_y - 1 + ab_lane % 4
     y = jnp.where(y < 0, y + ey, y)
     target = ((base_x + ab_lane // 4) * ey + y)[0:1]
@@ -233,8 +249,6 @@
     recv_faces(0)
     cur[...] = total[...]
     wait_sends(0)
-    grand = reduce_wait(0, 1)
-    scale = (ncells / grand)[0:1]
     lane = iota((ey, nz), 1)
     y_row = iota((ey, nz), 0)
     own_y = y_row < cy
@@ -260,7 +274,13 @@
     def down_z(v):
         return jnp.where(lane == 0, 0.0, pltpu.roll(v, 1, 1))
 
-    def forward(slot):
+    def scale():
+        value = red_src[0, 1]
+        for k in range(1, ny):
+            value = value + red_y[0, k - 1]
+        return (ncells / value)[0:1]
+
+    def forward(step):
         parts = [split(cur[c].reshape(rows, nz)) for c in range(comps)]
         stack = jnp.concatenate([p[0] for p in parts] + [p[1] for p in parts], axis=1)
         picked = mm(sel_t[...], stack).astype(BF16)
@@ -269,8 +289,7 @@
             r = slice(16 * b, 16 * (b + 1))
             hi = jnp.concatenate([picked[r, nz * c : nz * (c + 1)] for c in range(comps)], axis=0)
             lo = jnp.concatenate([picked[r, nz * (comps + c) : nz * (comps + c + 1)] for c in range(comps)], axis=0)
-            whi, wlo = wt_hi[b], wt_lo[b]
-            q = mm(hi, whi) + mm(lo, whi) + mm(hi, wlo)
+            q = folded(hi, lo, w_ahead[b])
             u = uv[b]
             alive = iota((1, 128), 1) < fill_ref[b]
             back = []
@@ -278,14 +297,20 @@
                 v = jnp.sum(q[16 * c : 16 * (c + 1)] * u, axis=0, keepdims=True)
                 mis = jnp.where(alive, v - targ_ref[c : c + 1, 128 * b : 128 * (b + 1)], 0.0)
                 data = data + mis * mis
-                back.append((mis * (2.0 * scale)) * u)
+                back.append((mis * 2.0) * u)
             dhi, dlo = split(jnp.concatenate(back, axis=0))
-            t = mm_nt(dhi, whi) + mm_nt(dlo, whi) + mm_nt(dhi, wlo)
+            t = folded(dhi, dlo, w_back[b])
             thi, tlo = split(t)
             for c in range(comps):
                 term[r, nz * c : nz * (c + 1)] = thi[16 * c : 16 * (c + 1)]
                 term[r, nz * (comps + c) : nz * (comps + c + 1)] = tlo[16 * c : 16 * (c + 1)]
         pulled = mm(sel[...], term[...])
+
+        @pl.when(step == 0)
+        def _():
+            reduce_wait(0, 1)
+
+        ratio = scale()
         spread = jnp.zeros((ey, nz), F32)
         div = []
         for x in range(1, cx + 1):
@@ -295,7 +320,7 @@
             spread = spread + dv * dv
             div.append(dv)
         for c in range(comps):
-            whole = pulled[:, nz * c : nz * (c + 1)] + pulled[:, nz * (comps + c) : nz * (comps + c + 1)]
+            whole = ratio * (pulled[:, nz * c : nz * (c + 1)] + pulled[:, nz * (comps + c) : nz * (comps + c + 1)])
             for x in range(ex):
                 value = whole[ey * x : ey * (x + 1)]
                 if c == 0:
@@ -310,7 +335,7 @@
                     else:
                         value = value + penalty_weight * (down_z(dv) - up_z(dv))
                 grad[c, x] = value
-        return data * (scale / ncells) + (penalty_weight / ncells) * jnp.sum(spread, axis=0, keepdims=True)
+        return data * (ratio / ncells) + (penalty_weight / ncells) * jnp.sum(spread, axis=0, keepdims=True)
 
     def update(step):
         def pick(values):
@@ -333,17 +358,18 @@
     def body(step, losses):
         loss = forward(step)
         losses = jnp.where(sub == step, loss, losses)
-        send_faces(step + 1)
 
         @pl.when(step == ITERS - 1)
         def _():
             reduce_start(1, 0, losses)
 
-        recv_faces(step + 1)
+        send_faces(step + 1)
 
         @pl.when(step == ITERS - 1)
         def _():
             reduce_start(1, 1, reduce_wait(1, 0))
+
+        recv_faces(step + 1)
 
         update(step)
         wait_sends(step + 1)
@@ -372,12 +398,18 @@
             jax.ShapeDtypeStruct(coefficients.shape, F32),
             jax.ShapeDtypeStruct((ITERS,), F32),
         ),
-        in_specs=[smem, smem, vmem, vmem, vmem],
+        in_specs=[pl.BlockSpec(memory_space=pltpu.HBM)] * 5,
         out_specs=(vmem, smem),
         scratch_shapes=[
+            pltpu.SMEM((blocks,), jnp.int32),
+            pltpu.SMEM((blocks,), jnp.int32),
+            pltpu.VMEM(coefficients.shape, F32),
+            pltpu.VMEM(fractions.shape, F32),
+            pltpu.VMEM(targets.shape, F32),
+            dma((5,)),
             state, state, state, state, state,
-            pltpu.VMEM((blocks, nz, 128), BF16),
-            pltpu.VMEM((blocks, nz, 128), BF16),
+            pltpu.VMEM((blocks, 2 * nz, 256), BF16),
+            pltpu.VMEM((blocks, 256, 2 * nz), BF16),
             pltpu.VMEM((blocks, 16, 128), F32),
             pltpu.VMEM((rows, 16 * blocks), BF16),
             pltpu.VMEM((16 * blocks, rows), BF16),
@@ -395,7 +427,7 @@
             dma((2, ny - 1)), dma((2, ny - 1)),
         ],
         compiler_params=pltpu.CompilerParams(
-            collective_id=0, has_side_effects=True, vmem_limit_bytes=32 * 1024 * 1024
+            collective_id=0, has_side_effects=True, vmem_limit_bytes=60 * 1024 * 1024
         ),
     )(block_cell, block_fill, coefficients, fractions, targets)
 

time: 53.8 us -> 42 us (0.78)
  Pallas kernels: 48 us -> 39.1 us
  local copies, waits for them, and re-layouts: 4.86 us -> 2.06 us
    pallas_call x1, Pallas kernels: 48 us -> 39.1 us  [shards(): pl.pallas_call(functools.partial(kernel, nx, ny), out_shape=(jax.ShapeDty...]
    unnamed x12 -> x4, local copies, waits for them, and re-layouts: 4.86 us -> 2.06 us
where the time goes in v2:
time: 42 us; the launch traced here: 41.8 us
  Pallas kernels  39.1 us (93%)
  local copies, waits for them, and re-layouts  2.06 us (5%)
  between operations  0.65 us (2%)
    pallas_call x1, Pallas kernels, shards(): pl.pallas_call(functools.partial(kernel, nx, ny), out_shape=(jax.ShapeDty...  39.1 us
    unnamed x4, local copies, waits for them, and re-layouts  2.06 us

profile of v2, /device:TPU:0, one launch (start us, length us, event | category | flops | bytes accessed | tf_op | source)
XLA Modules:
  0.0 41.8 jit_solution(10244820707548482496)
XLA Ops:
  0.6 39.1 %shard_map.68 = (f32[3,4,16,128]{3,2,1,0:T(8,128)}, f32[4]{0:T(128)}) custom-call(s32[16]{0:T(128)} %cell_in.1, s32[16]{0:T(128)} %fill_in.1, f32[3,4,16,128]{3,2,1,0:T(8,128)} %coef_in.1, f32[3,2048]{1,0:T(4,128)} %frac_in.1, f32[3,2048]{1,0:T(4,128)} %targ_in.1), custom_call_target="tpu_custom_call" | custom-call | tf_op jit(solution)/shard_map/pallas_call | solution.py:395
  39.7 0.0 copy-start
  39.7 1.5 %copy.9 = f32[3,4,16,128]{3,2,1,0:T(8,128)} copy(f32[3,4,16,128]{3,2,1,0:T(8,128)} %get-tuple-element.4) | data formatting | bytes 196608
  41.3 0.0 copy-done
  41.3 0.5 %copy.10 = f32[4]{0:T(128)} copy(f32[4]{0:T(128)S(1)} %copy-done) | data formatting | bytes 32
Async XLA Ops:
  39.7 1.6 %copy-start = (f32[4]{0:T(128)S(1)}, f32[4]{0:T(128)}, u32[]{:S(2)}) copy-start(f32[4]{0:T(128)} %get-tuple-element.5) | copy-start | bytes 52

commit v3 on v2

--- a/solution.py
+++ b/solution.py
@@ -132,10 +132,6 @@
     sub = iota((8, nz), 0)
 
     def send_faces(slot):
-        for n in range(2):
-            @pl.when(can_send[n])
-            def _():
-                face_copy(n, slot).start()
         for side in range(2):
             tiles = []
             for c in range(comps):
@@ -151,7 +147,7 @@
                 late = min(j + 5, 8)
                 sc[2 * side, j] = jnp.where(sub < 4, turned[j], tiles[late])
                 sc[2 * side + 1, j] = jnp.where(sub < 4, tiles[j], turned[late])
-        for n in range(2, 8):
+        for n in (4, 5, 6, 7, 2, 3, 0, 1):
             @pl.when(can_send[n])
             def _():
                 face_copy(n, slot).start()

time: 42 us -> 41.5 us (0.988)
  Pallas kernels: 39.1 us -> 38.6 us
    pallas_call x1, Pallas kernels: 39.1 us -> 38.6 us  [shards(): pl.pallas_call(functools.partial(kernel, nx, ny), out_shape=(jax.ShapeDty...]
where the time goes in v3:
time: 41.5 us; the launch traced here: 41.3 us
  Pallas kernels  38.6 us (93%)
  local copies, waits for them, and re-layouts  2.06 us (5%)
  between operations  0.65 us (2%)
    pallas_call x1, Pallas kernels, shards(): pl.pallas_call(functools.partial(kernel, nx, ny), out_shape=(jax.ShapeDty...  38.6 us
    unnamed x4, local copies, waits for them, and re-layouts  2.06 us

profile of v3, /device:TPU:0, one launch (start us, length us, event | category | flops | bytes accessed | tf_op | source)
XLA Modules:
  0.0 41.3 jit_solution(2456947954980641567)
XLA Ops:
  0.6 38.6 %shard_map.68 = (f32[3,4,16,128]{3,2,1,0:T(8,128)}, f32[4]{0:T(128)}) custom-call(s32[16]{0:T(128)} %cell_in.1, s32[16]{0:T(128)} %fill_in.1, f32[3,4,16,128]{3,2,1,0:T(8,128)} %coef_in.1, f32[3,2048]{1,0:T(4,128)} %frac_in.1, f32[3,2048]{1,0:T(4,128)} %targ_in.1), custom_call_target="tpu_custom_call" | custom-call | tf_op jit(solution)/shard_map/pallas_call | solution.py:391
  39.2 0.0 copy-start
  39.2 1.5 %copy.9 = f32[3,4,16,128]{3,2,1,0:T(8,128)} copy(f32[3,4,16,128]{3,2,1,0:T(8,128)} %get-tuple-element.4) | data formatting | bytes 196608
  40.8 0.0 copy-done
  40.8 0.5 %copy.10 = f32[4]{0:T(128)} copy(f32[4]{0:T(128)S(1)} %copy-done) | data formatting | bytes 32
Async XLA Ops:
  39.2 1.6 %copy-start = (f32[4]{0:T(128)S(1)}, f32[4]{0:T(128)}, u32[]{:S(2)}) copy-start(f32[4]{0:T(128)} %get-tuple-element.5) | copy-start | bytes 52
